TPU v7x, 32 devices: a whole 2x2x4 slice. The times are simulated.
32 devices in a mesh: members: 2 (over x), cols: 16 (over z, y, core).
Axes of the slice: x: 2, y: 2, z: 4, core: 2. Of those that a mesh axis runs over, the one named last changes fastest.
Arguments:
- adj_in: float32 [128, 5, 32, 1024], P(('members', 'cols')), parts along dimension 0, may hold values from -4 to 5
- courant_x: float32 [128, 32, 1024], P(('members', 'cols')), parts along dimension 0, may hold values from 0.05 to 0.45
- courant_y: float32 [128, 32, 1024], P(('members', 'cols')), parts along dimension 0, may hold values from 0.05 to 0.45
- spread: float32 [64, 32, 1024], P('cols'), may hold values from 0.5 to 2
- corr_band: float32 [5, 32, 32], replicated, may hold values from 0 to 1.5, as said below
- jacobian: bfloat16 [4096, 160, 128], P(('members', 'cols')), parts along dimension 0, may hold values from -0.5 to 0.5
- departures: bfloat16 [4096, 128], P(('members', 'cols')), parts along dimension 0, may hold values from -6 to 6
- obs_owner: int32 [4096], P(('members', 'cols')), parts along dimension 0, may hold values from 0 to 15, as said below
- obs_cell: int32 [4096], P(('members', 'cols')), parts along dimension 0, may hold values from 0 to 4095
- obs_count: int32 [4096], P(('members', 'cols')), parts along dimension 0, may hold values from 32 to 128
Outputs:
- gradient: float32 [128, 5, 32, 1024], P(('members', 'cols')), parts along dimension 0
There are 2 independent parts, one for each index of `members`. A program takes and returns all parts, laid end to end along the dimension named above; an argument that names none is the same for every part. Nothing has to cross between parts.
Inputs may be any that keep to these rules, and one draw needn't show every extreme that they name: corr_band is symmetric in its last two dimensions and zero more than 4 levels from the diagonal. `obs_owner`: among one device's 128 panels no tile is named more than 16 times; in every draw one tile is named exactly 16 times by every device's panels.
All inputs are finite; a program needn't handle non-finite values.
Results may differ from a plain program's by a relative error of at most 0.0003.
Values sent between devices are 32-bit elements; how exact they have to be, the bound alone decides.
A program may use at most 64 MiB of HBM per device.

v0:
```python
import jax
import jax.numpy as jnp
from jax import lax
from jax.sharding import PartitionSpec as P

STEPS = 8


def shifted(value, axis, steps):
    count = lax.axis_size(axis)
    pairs = [(source, (source + steps) % count) for source in range(count)]
    return lax.ppermute(value, axis, pairs)


def step_rows(adjoint, ahead, courant_x, courant_y):
    ahead_y = jnp.roll(adjoint, -1, axis=3)
    return (
        adjoint + courant_x[:, None] * (ahead - adjoint) + courant_y[:, None] * (ahead_y - adjoint)
    )


def per_device(
    adj_in,
    courant_x,
    courant_y,
    spread,
    corr_band,
    jacobian,
    departures,
    obs_owner,
    obs_cell,
    obs_count,
):
    strip_rows, fields, levels, cycle_cells = adj_in.shape
    panels_dev, field_levels, channels = jacobian.shape
    adjoint = adj_in
    for advect_step in range(STEPS):
        border = shifted(adjoint[0:1], "cols", -1)
        ahead = jnp.concatenate([adjoint[1:], border], 0)
        adjoint = step_rows(adjoint, ahead, courant_x, courant_y)
    channel = jnp.arange(channels, dtype=jnp.int32)
    masked = jnp.where(
        channel[None, :] < obs_count[:, None], departures, jnp.zeros((), departures.dtype)
    )
    obs_grad = jnp.einsum("pkc,pc->pk", jacobian, masked, preferred_element_type=jnp.float32)
    n_cols = lax.axis_size("cols")
    capacity = 2 * panels_dev // n_cols
    total_slots = n_cols * capacity
    row_ids = jnp.arange(panels_dev, dtype=jnp.int32)
    earlier = (obs_owner[:, None] == obs_owner[None, :]) & (row_ids[None, :] < row_ids[:, None])
    position = jnp.sum(earlier.astype(jnp.int32), axis=1)
    slot_index = obs_owner * capacity + position
    placing = slot_index[:, None] == jnp.arange(total_slots, dtype=jnp.int32)[None, :]
    send_grad = jnp.einsum(
        "ps,pk->sk", placing.astype(jnp.float32), obs_grad, precision=lax.Precision.HIGHEST
    )
    send_cell = jnp.sum(jnp.where(placing, obs_cell[:, None] + 1, 0), axis=0) - 1
    recv_grad, recv_cell = (
        lax.all_to_all(
            send_grad.reshape(n_cols, capacity * field_levels),
            "cols",
            split_axis=0,
            concat_axis=0,
            tiled=True,
        ),
        lax.all_to_all(
            send_cell.reshape(n_cols, capacity), "cols", split_axis=0, concat_axis=0, tiled=True
        ),
    )
    slot_grad = recv_grad.reshape(total_slots, field_levels)
    slot_cell = recv_cell.reshape(total_slots)
    row_hit = (
        slot_cell[:, None] // cycle_cells == jnp.arange(strip_rows, dtype=jnp.int32)[None, :]
    ).astype(jnp.float32)
    col_hit = (
        slot_cell[:, None] % cycle_cells == jnp.arange(cycle_cells, dtype=jnp.int32)[None, :]
    ).astype(jnp.float32)
    spread_grad = slot_grad[:, None, :] * row_hit[:, :, None]
    increment = jnp.einsum("sxk,sy->xky", spread_grad, col_hit, precision=lax.Precision.HIGHEST)
    total = adjoint + increment.reshape(strip_rows, fields, levels, cycle_cells)
    scaled = spread[:, None] * total
    mixed = jnp.einsum("flk,xfky->xfly", corr_band, scaled, precision=lax.Precision.HIGHEST)
    return spread[:, None] * mixed


def solution(mesh):
    in_specs = (
        P(("members", "cols"), None, None, None),
        P(("members", "cols"), None, None),
        P(("members", "cols"), None, None),
        P("cols", None, None),
        P(),
        P(("members", "cols"), None, None),
        P(("members", "cols"), None),
        P(("members", "cols")),
        P(("members", "cols")),
        P(("members", "cols")),
    )
    out_specs = P(("members", "cols"), None, None, None)
    return jax.shard_map(
        per_device, mesh=mesh, in_specs=in_specs, out_specs=out_specs, check_vma=False
    )
```

profile of v0, /device:TPU:29, one launch (start us, length us, event | category | flops | bytes accessed | tf_op | source)
XLA Modules:
  0.0 130.3 jit_solution(7051241290474802096)
XLA Ops:
  0.0 1.2 slice.131
  1.2 0.1 copy.72
  1.3 0.7 collective-permute-start
  2.0 12.0 %collective-permute-done = f32[1,5,32,1024]{3,2,0,1:T(8,128)S(1)} collective-permute-done((f32[1,5,32,1024]{3,2,0,1:T(8,128)S(1)}, f32[1,5,32,1024]{3,2,0,1:T(8,128)S(1)}, u32[]{:S(2)}, u32[]{:S(2)}) %collective-permute-start) | collective-permute-done | bytes 655392 | tf_op jit(solution)/shard_map/ppermute | solution.py:12
  14.1 4.3 %fusion.2 = f32[4,5,32,1024]{3,2,0,1:T(8,128)S(1)} fusion(f32[1,5,32,1024]{3,2,0,1:T(8,128)S(1)} %collective-permute-done, f32[4,32,1024]{2,1,0:T(8,128)S(1)} %copy-done.4, f32[4,32,1024]{2,1,0:T(8,128)S(1)} %copy-done.5, f32[4,5,32,1024]{3,2,1,0:T(8,128)} %param.10), kind=kLoop, calls=%fused_computation.3 | loop fusion | flops 5242880 | bytes 11862016 | tf_op jit(solution)/shard_map/add | solution.py:18
  18.4 0.1 slice.135
  18.4 0.1 collective-permute-start.1
  18.5 0.2 slice.134
  18.8 0.7 slice.136
  19.5 11.7 %collective-permute-done.1 = f32[1,5,32,1024]{3,2,0,1:T(8,128)S(1)} collective-permute-done((f32[1,5,32,1024]{3,2,0,1:T(8,128)S(1)}, f32[1,5,32,1024]{3,2,0,1:T(8,128)S(1)}, u32[]{:S(2)}, u32[]{:S(2)}) %collective-permute-start.1) | collective-permute-done | bytes 655392 | tf_op jit(solution)/shard_map/ppermute | solution.py:12
  31.2 1.3 fusion.6
  32.5 0.1 slice.139
  32.6 0.1 collective-permute-start.2
  32.7 0.2 slice.138
  32.9 0.7 slice.140
  33.6 11.7 %collective-permute-done.2 = f32[1,5,32,1024]{3,2,0,1:T(8,128)S(1)} collective-permute-done((f32[1,5,32,1024]{3,2,0,1:T(8,128)S(1)}, f32[1,5,32,1024]{3,2,0,1:T(8,128)S(1)}, u32[]{:S(2)}, u32[]{:S(2)}) %collective-permute-start.2) | collective-permute-done | bytes 655392 | tf_op jit(solution)/shard_map/ppermute | solution.py:12
  45.3 1.3 fusion.10
  46.6 0.1 slice.143
  46.7 0.1 collective-permute-start.3
  46.8 0.2 slice.142
  47.0 0.7 slice.144
  47.8 11.7 %collective-permute-done.3 = f32[1,5,32,1024]{3,2,0,1:T(8,128)S(1)} collective-permute-done((f32[1,5,32,1024]{3,2,0,1:T(8,128)S(1)}, f32[1,5,32,1024]{3,2,0,1:T(8,128)S(1)}, u32[]{:S(2)}, u32[]{:S(2)}) %collective-permute-start.3) | collective-permute-done | bytes 655392 | tf_op jit(solution)/shard_map/ppermute | solution.py:12
  59.4 1.3 fusion.14
  60.8 0.1 slice.147
  60.8 0.1 collective-permute-start.4
  60.9 0.2 slice.146
  61.2 0.7 slice.148
  61.9 11.7 %collective-permute-done.4 = f32[1,5,32,1024]{3,2,0,1:T(8,128)S(1)} collective-permute-done((f32[1,5,32,1024]{3,2,0,1:T(8,128)S(1)}, f32[1,5,32,1024]{3,2,0,1:T(8,128)S(1)}, u32[]{:S(2)}, u32[]{:S(2)}) %collective-permute-start.4) | collective-permute-done | bytes 655392 | tf_op jit(solution)/shard_map/ppermute | solution.py:12
  73.6 1.1 fusion.18
  74.7 1.0 slice.151
  75.7 0.2 convert_reduce_fusion
  75.9 0.1 select_reduce_fusion
  76.0 0.7 sub.77
  76.7 7.8 %all-to-all-start.1 = ((s32[16,1,16]{2,1,0:T(1,128)}), s32[16,1,16]{2,1,0:T(1,128)S(1)}, u32[]{:S(2)}, u32[]{:S(2)}) async-start(s32[16,1,16]{2,1,0:T(1,128)} %sub.77), calls=%async_computation.1 | async-start | bytes 16384 | tf_op jit(solution)/shard_map/all_to_all | solution.py:66
  84.6 0.1 slice.150
  84.8 0.0 slice-start.2
  84.8 0.7 slice.152
  85.5 0.0 slice-start.3
  85.6 3.3 %collective-permute-done.5 = f32[1,5,32,1024]{3,2,0,1:T(8,128)} collective-permute-done((f32[1,5,32,1024]{3,2,0,1:T(8,128)}, f32[1,5,32,1024]{3,2,0,1:T(8,128)}, u32[]{:S(2)}, u32[]{:S(2)}) %collective-permute-start.5) | collective-permute-done | bytes 655392 | tf_op jit(solution)/shard_map/ppermute | solution.py:12
  88.9 3.0 %fusion.22 = f32[4,5,32,1024]{3,2,0,1:T(8,128)S(1)} fusion(f32[4,5,32,1024]{3,2,0,1:T(8,128)} %copy-done.3, f32[1,5,32,1024]{3,2,0,1:T(8,128)} %collective-permute-done.5, f32[3,5,32,1024]{3,2,0,1:T(8,128)S(1)} %slice.150, f32[4,5,32,1]{3,2,0,1:T(8,128)S(1)} %slice.153, f32[4,5,32,1023]{3,2,0,1:T(8,128)S(1)} %slice.152, f32[4,32,1024]{2,1,0:T(8,128)S(1)} %copy-done.4, ...), kind=kLoop, calls=%fused_computation.33 | loop fusion | flops 5242880 | bytes 11534336 | tf_op jit(solution)/shard_map/add | solution.py:18
  91.9 0.9 slice.155
  92.8 0.1 fusion.63
  92.9 2.8 %fusion.58 = f32[128,1,160]{2,1,0:T(1,128)S(1)} fusion(bf16[128,160,128]{2,1,0:T(8,128)(2,1)S(1)} %bitcast.19, bf16[128,128,1]{1,0,2:T(8,128)(2,1)S(1)} %fusion.63), kind=kOutput, calls=%fused_computation.73 | convolution fusion | flops 5242880 | bytes 5357568 | tf_op jit(solution)/shard_map/pkc,pc->pk/dot_general | solution.py:45
  95.7 0.4 fusion.54
  96.1 1.0 all_to_all.13
  97.1 7.9 %all-to-all-start = ((f32[16,1,2560]{2,1,0:T(1,128)}), f32[16,1,2560]{2,1,0:T(1,128)S(1)}, u32[]{:S(2)}, u32[]{:S(2)}) async-start(f32[16,1,2560]{2,1,0:T(1,128)} %all_to_all.13), calls=%async_computation | async-start | bytes 327680 | tf_op jit(solution)/shard_map/all_to_all | solution.py:59
  104.9 0.5 broadcast.130
  105.5 0.7 reduce.4
  106.1 0.1 broadcast_in_dim_reshape.2
  106.3 0.1 slice.154
  106.4 0.7 slice.156
  107.2 0.3 copy-done.7
  107.5 2.2 %fusion.26 = f32[4,5,32,1024]{3,2,0,1:T(8,128)S(1)} fusion(f32[4,5,32,1024]{3,2,0,1:T(8,128)S(1)} %fusion.22, f32[1,5,32,1024]{3,2,0,1:T(8,128)} %collective-permute-done.6, f32[3,5,32,1024]{3,2,0,1:T(8,128)S(1)} %slice.154, f32[4,5,32,1]{3,2,0,1:T(8,128)S(1)} %slice.157, f32[4,5,32,1023]{3,2,0,1:T(8,128)S(1)} %slice.156, f32[4,32,1024]{2,1,0:T(8,128)S(1)} %copy-done.4, ...), kind=kLoop, calls=%fused_computation.39 | loop fusion | flops 5242880 | bytes 11534336 | tf_op jit(solution)/shard_map/add | solution.py:18
  109.7 1.5 %copy-done.1 = f32[4,5,32,1024]{3,2,0,1:T(8,128)} copy-done((f32[4,5,32,1024]{3,2,0,1:T(8,128)}, f32[4,5,32,1024]{3,2,0,1:T(8,128)S(1)}, u32[]{:S(2)}) %copy-start.1) | copy-done | bytes 2621464
  111.2 0.6 collective-permute-start.7
  111.9 0.4 reduce
  112.3 0.1 mul.75
  112.4 0.1 copy.52
  112.5 1.4 %fusion.48 = f32[4,160,1024]{2,1,0:T(8,128)S(1)} fusion(s32[256]{0:T(256)S(1)} %get-tuple-element.6, f32[256,4]{0,1:T(4,128)S(1)} %fusion.64, f32[256,160]{0,1:T(8,128)S(1)} %copy.52), kind=kOutput, calls=%fused_computation.62 | convolution fusion | flops 2013691904 | bytes 2790400 | tf_op jit(solution)/shard_map/sxk,sy->xky/dot_general | solution.py:79
  114.0 1.7 %copy-done.2 = f32[4,5,32,1024]{3,2,0,1:T(8,128)S(1)} copy-done((f32[4,5,32,1024]{3,2,0,1:T(8,128)S(1)}, f32[4,5,32,1024]{3,2,0,1:T(8,128)}, u32[]{:S(2)}) %copy-start.2) | copy-done | bytes 2621464
  115.7 0.7 slice.160
  116.5 7.7 %collective-permute-done.7 = f32[1,5,32,1024]{3,2,0,1:T(8,128)S(1)} collective-permute-done((f32[1,5,32,1024]{3,2,0,1:T(8,128)S(1)}, f32[1,5,32,1024]{3,2,0,1:T(8,128)S(1)}, u32[]{:S(2)}, u32[]{:S(2)}) %collective-permute-start.7) | collective-permute-done | bytes 655392 | tf_op jit(solution)/shard_map/ppermute | solution.py:12
  124.2 4.2 %bitcast_multiply_fusion = f32[4,5,32,1024]{3,2,0,1:T(8,128)S(1)} fusion(f32[4,5,32,1024]{3,2,0,1:T(8,128)S(1)} %copy-done.2, f32[1,5,32,1024]{3,2,0,1:T(8,128)S(1)} %collective-permute-done.7, f32[3,5,32,1024]{3,2,0,1:T(8,128)S(1)} %slice-done.1, f32[4,5,32,1]{3,2,0,1:T(8,128)S(1)} %slice-done, f32[4,5,32,1023]{3,2,0,1:T(8,128)S(1)} %slice.160, ...), kind=kOutput, calls=%fused_computation.55 | convolution fusion | flops 258867200 | bytes 14700544 | tf_op jit(solution)/shard_map/flk,xfky->xfly/dot_general | solution.py:82
  128.4 1.8 %copy.54 = f32[4,5,32,1024]{3,2,1,0:T(8,128)} copy(f32[4,5,32,1024]{3,2,0,1:T(8,128)S(1)} %bitcast_multiply_fusion) | data formatting | bytes 5242880 | tf_op jit(solution)/shard_map/mul | solution.py:83
  (48 shorter events, 0.4 us)
Async XLA Ops:
  0.0 124.2 %copy-start = (f32[5,32,32]{2,1,0:T(8,128)S(1)}, f32[5,32,32]{2,1,0:T(8,128)}, u32[]{:S(2)}) copy-start(f32[5,32,32]{2,1,0:T(8,128)} %param.14) | copy-start | bytes 61444
  0.0 14.1 %copy-start.4 = (f32[4,32,1024]{2,1,0:T(8,128)S(1)}, f32[4,32,1024]{2,1,0:T(8,128)}, u32[]{:S(2)}) copy-start(f32[4,32,1024]{2,1,0:T(8,128)} %param.12) | copy-start | bytes 1572868
  0.0 14.1 %copy-start.5 = (f32[4,32,1024]{2,1,0:T(8,128)S(1)}, f32[4,32,1024]{2,1,0:T(8,128)}, u32[]{:S(2)}) copy-start(f32[4,32,1024]{2,1,0:T(8,128)} %param.11) | copy-start | bytes 1572868
  1.3 12.8 %collective-permute-start = (f32[1,5,32,1024]{3,2,0,1:T(8,128)S(1)}, f32[1,5,32,1024]{3,2,0,1:T(8,128)S(1)}, u32[]{:S(2)}, u32[]{:S(2)}) collective-permute-start(f32[1,5,32,1024]{3,2,0,1:T(8,128)S(1)} %copy.72), channel_id=1, source_target_pairs={{0,15},{1,0},{2,1},{3,2},{4,3},{5,4},{6,5},{7,6},{8,7},{9,8},{10,9... | collective-permute-start | bytes 1966088 | tf_op jit(solution)/shard_map/ppermute | solution.py:12
  18.4 12.8 %collective-permute-start.1 = (f32[1,5,32,1024]{3,2,0,1:T(8,128)S(1)}, f32[1,5,32,1024]{3,2,0,1:T(8,128)S(1)}, u32[]{:S(2)}, u32[]{:S(2)}) collective-permute-start(f32[1,5,32,1024]{3,2,0,1:T(8,128)S(1)} %slice.135), channel_id=1, source_target_pairs={{0,15},{1,0},{2,1},{3,2},{4,3},{5,4},{6,5},{7,6},{8,7},{9,8},{10,9... | collective-permute-start | bytes 1966088 | tf_op jit(solution)/shard_map/ppermute | solution.py:12
  32.6 12.8 %collective-permute-start.2 = (f32[1,5,32,1024]{3,2,0,1:T(8,128)S(1)}, f32[1,5,32,1024]{3,2,0,1:T(8,128)S(1)}, u32[]{:S(2)}, u32[]{:S(2)}) collective-permute-start(f32[1,5,32,1024]{3,2,0,1:T(8,128)S(1)} %slice.139), channel_id=1, source_target_pairs={{0,15},{1,0},{2,1},{3,2},{4,3},{5,4},{6,5},{7,6},{8,7},{9,8},{10,9... | collective-permute-start | bytes 1966088 | tf_op jit(solution)/shard_map/ppermute | solution.py:12
  46.7 12.8 %collective-permute-start.3 = (f32[1,5,32,1024]{3,2,0,1:T(8,128)S(1)}, f32[1,5,32,1024]{3,2,0,1:T(8,128)S(1)}, u32[]{:S(2)}, u32[]{:S(2)}) collective-permute-start(f32[1,5,32,1024]{3,2,0,1:T(8,128)S(1)} %slice.143), channel_id=1, source_target_pairs={{0,15},{1,0},{2,1},{3,2},{4,3},{5,4},{6,5},{7,6},{8,7},{9,8},{10,9... | collective-permute-start | bytes 1966088 | tf_op jit(solution)/shard_map/ppermute | solution.py:12
  60.8 12.8 %collective-permute-start.4 = (f32[1,5,32,1024]{3,2,0,1:T(8,128)S(1)}, f32[1,5,32,1024]{3,2,0,1:T(8,128)S(1)}, u32[]{:S(2)}, u32[]{:S(2)}) collective-permute-start(f32[1,5,32,1024]{3,2,0,1:T(8,128)S(1)} %slice.147), channel_id=1, source_target_pairs={{0,15},{1,0},{2,1},{3,2},{4,3},{5,4},{6,5},{7,6},{8,7},{9,8},{10,9... | collective-permute-start | bytes 1966088 | tf_op jit(solution)/shard_map/ppermute | solution.py:12
  61.9 13.8 %copy-start.12 = (s32[128]{0:T(128)S(1)}, s32[128]{0:T(128)}, u32[]{:S(2)}) copy-start(s32[128]{0:T(128)} %param.17) | copy-start | bytes 1540
  61.9 14.0 %copy-start.13 = (s32[128]{0:T(128)S(1)}, s32[128]{0:T(128)}, u32[]{:S(2)}) copy-start(s32[128]{0:T(128)} %param.18) | copy-start | bytes 1540
  74.7 10.0 %copy-start.3 = (f32[4,5,32,1024]{3,2,0,1:T(8,128)}, f32[4,5,32,1024]{3,2,0,1:T(8,128)S(1)}, u32[]{:S(2)}) copy-start(f32[4,5,32,1024]{3,2,0,1:T(8,128)S(1)} %fusion.18) | copy-start | bytes 7864324
  75.7 13.2 %collective-permute-start.5 = (f32[1,5,32,1024]{3,2,0,1:T(8,128)}, f32[1,5,32,1024]{3,2,0,1:T(8,128)}, u32[]{:S(2)}, u32[]{:S(2)}) collective-permute-start(f32[1,5,32,1024]{3,2,0,1:T(8,128)} %slice.151), channel_id=1, source_target_pairs={{0,15},{1,0},{2,1},{3,2},{4,3},{5,4},{6,5},{7,6},{8,7},{9,8},{10,9... | collective-permute-start | bytes 1966088 | tf_op jit(solution)/shard_map/ppermute | solution.py:12
  76.7 20.4 %all-to-all-start.1 = ((s32[16,1,16]{2,1,0:T(1,128)}), s32[16,1,16]{2,1,0:T(1,128)S(1)}, u32[]{:S(2)}, u32[]{:S(2)}) async-start(s32[16,1,16]{2,1,0:T(1,128)} %sub.77), calls=%async_computation.1 | async-start | bytes 16384 | tf_op jit(solution)/shard_map/all_to_all | solution.py:66
  84.8 4.1 %copy-start.6 = (f32[4,32,1024]{2,1,0:T(8,128)S(1)}, f32[4,32,1024]{2,1,0:T(8,128)}, u32[]{:S(2)}) copy-start(f32[4,32,1024]{2,1,0:T(8,128)} %param.11) | copy-start | bytes 1572868
  84.8 8.1 %slice-start.2 = ((s8[5242880]{0:T(1024)(128)(4,1)}), s8[4194304]{0:T(1024)(128)(4,1)S(1)}, s32[]{:S(2)}) async-start(s8[5242880]{0:T(1024)(128)(4,1)} %bitcast.18), calls=%async_computation.4 | async-start | bytes 8388608
  85.5 7.3 %copy-start.10 = (bf16[128,128]{1,0:T(8,128)(2,1)S(1)}, bf16[128,128]{1,0:T(8,128)(2,1)}, u32[]{:S(2)}) copy-start(bf16[128,128]{1,0:T(8,128)(2,1)} %param.16) | copy-start | bytes 98308
  85.5 7.2 %copy-start.11 = (s32[128]{0:T(128)S(1)}, s32[128]{0:T(128)}, u32[]{:S(2)}) copy-start(s32[128]{0:T(128)} %param.19) | copy-start | bytes 1540
  85.5 7.3 %slice-start.3 = ((s8[5242880]{0:T(1024)(128)(4,1)}), s8[1048576]{0:T(1024)(128)(4,1)S(1)}, s32[]{:S(2)}) async-start(s8[5242880]{0:T(1024)(128)(4,1)} %bitcast.18), calls=%async_computation.5 | async-start | bytes 2097152
  92.8 14.4 %collective-permute-start.6 = (f32[1,5,32,1024]{3,2,0,1:T(8,128)}, f32[1,5,32,1024]{3,2,0,1:T(8,128)}, u32[]{:S(2)}, u32[]{:S(2)}) collective-permute-start(f32[1,5,32,1024]{3,2,0,1:T(8,128)} %slice.155), channel_id=1, source_target_pairs={{0,15},{1,0},{2,1},{3,2},{4,3},{5,4},{6,5},{7,6},{8,7},{9,8},{10,9... | collective-permute-start | bytes 1966088 | tf_op jit(solution)/shard_map/ppermute | solution.py:12
  97.1 14.8 %all-to-all-start = ((f32[16,1,2560]{2,1,0:T(1,128)}), f32[16,1,2560]{2,1,0:T(1,128)S(1)}, u32[]{:S(2)}, u32[]{:S(2)}) async-start(f32[16,1,2560]{2,1,0:T(1,128)} %all_to_all.13), calls=%async_computation | async-start | bytes 327680 | tf_op jit(solution)/shard_map/all_to_all | solution.py:59
  106.4 1.0 copy-start.7
  109.7 1.5 %copy-start.1 = (f32[4,5,32,1024]{3,2,0,1:T(8,128)}, f32[4,5,32,1024]{3,2,0,1:T(8,128)S(1)}, u32[]{:S(2)}) copy-start(f32[4,5,32,1024]{3,2,0,1:T(8,128)S(1)} %fusion.26) | copy-start | bytes 7864324
  111.2 13.0 %collective-permute-start.7 = (f32[1,5,32,1024]{3,2,0,1:T(8,128)S(1)}, f32[1,5,32,1024]{3,2,0,1:T(8,128)S(1)}, u32[]{:S(2)}, u32[]{:S(2)}) collective-permute-start(f32[1,5,32,1024]{3,2,0,1:T(8,128)S(1)} %slice.159), channel_id=1, source_target_pairs={{0,15},{1,0},{2,1},{3,2},{4,3},{5,4},{6,5},{7,6},{8,7},{9,8},{10,9... | collective-permute-start | bytes 1966088 | tf_op jit(solution)/shard_map/ppermute | solution.py:12
  114.0 1.7 %copy-start.2 = (f32[4,5,32,1024]{3,2,0,1:T(8,128)S(1)}, f32[4,5,32,1024]{3,2,0,1:T(8,128)}, u32[]{:S(2)}) copy-start(f32[4,5,32,1024]{3,2,0,1:T(8,128)} %copy-done.1) | copy-start | bytes 7864324
  115.7 8.5 %slice-start = ((f32[4,5,32,1024]{3,2,0,1:T(8,128)}), f32[4,5,32,1]{3,2,0,1:T(8,128)S(1)}, s32[]{:S(2)}) async-start(f32[4,5,32,1024]{3,2,0,1:T(8,128)} %copy-done.1), calls=%async_computation.2 | async-start | bytes 655360 | tf_op jit(solution)/shard_map/jit(_roll_static)/slice | solution.py:16
  115.7 8.5 %slice-start.1 = ((f32[4,5,32,1024]{3,2,0,1:T(8,128)}), f32[3,5,32,1024]{3,2,0,1:T(8,128)S(1)}, s32[]{:S(2)}) async-start(f32[4,5,32,1024]{3,2,0,1:T(8,128)} %copy-done.1), calls=%async_computation.3 | async-start | bytes 3932160 | tf_op jit(solution)/shard_map/slice | solution.py:39
  115.7 8.5 %copy-start.8 = (f32[4,32,1024]{2,1,0:T(8,128)S(1)}, f32[4,32,1024]{2,1,0:T(8,128)}, u32[]{:S(2)}) copy-start(f32[4,32,1024]{2,1,0:T(8,128)} %param.11) | copy-start | bytes 1572868
  115.7 8.5 %copy-start.9 = (f32[4,32,1024]{2,1,0:T(8,128)S(1)}, f32[4,32,1024]{2,1,0:T(8,128)}, u32[]{:S(2)}) copy-start(f32[4,32,1024]{2,1,0:T(8,128)} %param.13) | copy-start | bytes 1572868
where the time goes:
time: 131 us; the launch traced here: 130 us
  waiting for transfers between devices  69.8 us (53%)
  local copies, waits for them, and re-layouts  17.9 us (14%)
  starting transfers between devices  17.3 us (13%)
  other arithmetic  15.9 us (12%)
  matrix products  8.84 us (7%)
    ppermute x8, waiting for transfers between devices, shifted(): return lax.ppermute(value, axis, pairs)  69.8 us
    add x7, other arithmetic, step_rows(): adjoint + courant_x[:, None] * (ahead - adjoint)  14.5 us
    all_to_all x1, starting transfers between devices, per_device(): lax.all_to_all(send_grad.reshape(n_cols, capacity * field_levels), 'cols'...  7.86 us
    all_to_all x1, starting transfers between devices, per_device(): lax.all_to_all(send_cell.reshape(n_cols, capacity), 'cols', split_axis=0,...  7.83 us
    slice x15, local copies, waits for them, and re-layouts, step_rows(): ahead_y = jnp.roll(adjoint, -1, axis=3)  5.48 us
    dot_general x1, matrix products, per_device(): jnp.einsum('flk,xfky->xfly', corr_band, scaled, precision=lax.Precision.H...  4.21 us
    unnamed x33, local copies, waits for them, and re-layouts  3.63 us
    slice x8, local copies, waits for them, and re-layouts, per_device(): border = shifted(adjoint[0:1], 'cols', -1)  3.36 us
  transfers between devices with their start and end apart: 10, of which 7 were waited for; matrix products, arithmetic and copies ran while one was open for 16% of the time, Pallas kernels for 0%

commit v1 on v0

v1 whole, which is shorter than its diff:
```python
import functools
import jax
import jax.numpy as jnp
from jax import lax
from jax.experimental import pallas as pl
from jax.experimental.pallas import tpu as pltpu
from jax.sharding import PartitionSpec as P

STEPS = 8
SUB = 8


def pieces(value):
    high = value.astype(jnp.bfloat16)
    rest = value - high.astype(jnp.float32)
    middle = rest.astype(jnp.bfloat16)
    low = (rest - middle.astype(jnp.float32)).astype(jnp.bfloat16)
    return high, middle, low


def window_kernel(
    n_cols,
    cap,
    adj_hbm,
    cx_hbm,
    cy_hbm,
    spread_hbm,
    corr_hbm,
    jac_hbm,
    dep_hbm,
    owner_hbm,
    cell_hbm,
    count_hbm,
    out_hbm,
    state,
    history,
    border,
    cx,
    cy,
    spread,
    corr,
    jac,
    dep,
    owner,
    cell,
    count,
    masked,
    grad,
    send_slots,
    recv_slots,
    increment,
    result,
    local_sem,
    row_send_sem,
    row_recv_sem,
    slot_send_sem,
    slot_recv_sem,
    out_sem,
):
    rows, fields, levels, cells = state.shape
    panels, field_levels, channels = jac.shape
    slots, width = send_slots.shape
    me = lax.axis_index("cols")
    left = lax.rem(me + n_cols - 1, n_cols)

    barrier = pltpu.get_barrier_semaphore()

    @pl.loop(1, n_cols)
    def _(shift):
        pl.semaphore_signal(barrier, inc=1, device_id={"cols": lax.rem(me + shift, n_cols)})

    loads = [
        pltpu.make_async_copy(source, target, local_sem.at[number])
        for number, (source, target) in enumerate(
            [(adj_hbm.at[x], state.at[x]) for x in range(rows)]
            + [
                (cx_hbm, cx),
                (cy_hbm, cy),
                (dep_hbm, dep),
                (owner_hbm, owner),
                (cell_hbm, cell),
                (count_hbm, count),
                (jac_hbm, jac),
                (spread_hbm, spread),
                (corr_hbm, corr),
            ]
        )
    ]
    for load in loads:
        load.start()

    pl.semaphore_wait(barrier, n_cols - 1)

    def row_copy(time, field):
        source = adj_hbm.at[0, field] if time == 0 else history.at[time - 1, field]
        return pltpu.make_async_remote_copy(
            src_ref=source,
            dst_ref=border.at[time, field],
            send_sem=row_send_sem.at[time, field],
            recv_sem=row_recv_sem.at[time, field],
            device_id={"cols": left},
        )

    @pl.loop(0, fields)
    def _(field):
        row_copy(0, field).start()

    for load in loads[: rows + 2]:
        load.wait()

    def advance(x, strip, value, ahead):
        return (
            value
            + cx[x, strip] * (ahead - value)
            + cy[x, strip] * (pltpu.roll(value, cells - 1, 1) - value)
        )

    strips = [pl.ds(SUB * s, SUB) for s in range(levels // SUB)]

    for time in range(1, rows):

        @pl.loop(0, fields)
        def _(field):
            for strip in strips:
                for x in range(rows - time):
                    if x == 0 and time > 1:
                        value = history[time - 2, field, strip]
                    else:
                        value = state[x, field, strip]
                    new = advance(x, strip, value, state[x + 1, field, strip])
                    if x == 0:
                        history[time - 1, field, strip] = new
                    else:
                        state[x, field, strip] = new
            row_copy(time, field).start()

    for load in loads[rows + 2 :]:
        load.wait()
    first = lax.broadcasted_iota(jnp.int32, (panels, panels), 0)
    second = lax.broadcasted_iota(jnp.int32, (panels, panels), 1)

    def as_column(row):
        return jnp.sum(jnp.where(first == second, row, 0), axis=1, keepdims=True)

    lane = lax.broadcasted_iota(jnp.int32, (panels, channels), 1)
    masked[...] = jnp.where(lane < as_column(count[...]), dep[...].astype(jnp.float32), 0.0)
    grad[...] = jnp.zeros_like(grad)

    @pl.loop(0, panels // SUB)
    def _(group):
        start = pl.multiple_of(group * SUB, SUB)
        weights = masked[pl.ds(start, SUB), :].astype(jnp.bfloat16)
        row = lax.broadcasted_iota(jnp.int32, (SUB, field_levels), 0)
        total = jnp.zeros((SUB, field_levels), jnp.float32)
        for i in range(SUB):
            product = lax.dot_general(
                weights, jac[start + i], (((1,), (1,)), ((), ())), preferred_element_type=jnp.float32
            )
            total = jnp.where(row == i, product, total)
        grad[pl.ds(start, SUB), 0:field_levels] = total

    same = (as_column(owner[...]) == owner[...]) & (first < second)
    position = jnp.sum(same.astype(jnp.int32), axis=0, keepdims=True)
    slot = owner[...] * cap + position
    placing = slot == lax.broadcasted_iota(jnp.int32, (slots, panels), 0)
    placing_cell = jnp.sum(
        jnp.where(placing, (cell[...] + 1).astype(jnp.float32), 0.0), axis=1, keepdims=True
    )
    chosen = placing.astype(jnp.float32).astype(jnp.bfloat16)
    placed = sum(
        jnp.dot(chosen, piece, preferred_element_type=jnp.float32) for piece in pieces(grad[...])
    )
    column = lax.broadcasted_iota(jnp.int32, (slots, width), 1)
    send_slots[...] = jnp.where(column == field_levels, placing_cell, placed)

    def slot_block(ref, device):
        return ref.at[pl.ds(pl.multiple_of(device * cap, SUB), cap), :]

    def slot_send(shift):
        target = lax.rem(me + shift, n_cols)
        return pltpu.make_async_remote_copy(
            src_ref=slot_block(send_slots, target),
            dst_ref=slot_block(recv_slots, me),
            send_sem=slot_send_sem.at[shift],
            recv_sem=slot_recv_sem.at[shift],
            device_id={"cols": target},
        )

    def slot_receive(shift):
        return pltpu.make_async_remote_copy(
            src_ref=slot_block(send_slots, me),
            dst_ref=slot_block(recv_slots, lax.rem(me + n_cols - shift, n_cols)),
            send_sem=slot_send_sem.at[shift],
            recv_sem=slot_recv_sem.at[shift],
            device_id={"cols": left},
        )

    @pl.loop(1, n_cols)
    def _(shift):
        slot_send(shift).start()

    own = pl.ds(pl.multiple_of(me * cap, SUB), cap)
    recv_slots[own, :] = send_slots[own, :]

    def add_panels():
        @pl.loop(1, n_cols)
        def _(shift):
            slot_receive(shift).wait_recv()

        received = recv_slots[...]
        target = received[:, field_levels : field_levels + 1].astype(jnp.int32) - 1
        parts = pieces(jnp.transpose(received)[0:field_levels, :])
        for x in range(rows):
            y = lax.broadcasted_iota(jnp.int32, (slots, cells), 1) + x * cells
            hit = (target == y).astype(jnp.float32).astype(jnp.bfloat16)
            increment[x] = sum(
                jnp.dot(part, hit, preferred_element_type=jnp.float32) for part in parts
            )

    def finish(x, field):
        inside = pl.ds(pl.multiple_of(field * levels, SUB), levels)
        total = state[x, field] + increment[x, inside, :]
        mixed = jnp.dot(
            corr[field],
            spread[x] * total,
            precision=lax.Precision.HIGHEST,
            preferred_element_type=jnp.float32,
        )
        result[x, field] = spread[x] * mixed
        out_copy(x, field).start()

    def out_copy(x, field):
        return pltpu.make_async_copy(result.at[x, field], out_hbm.at[x, field], out_sem.at[x, field])

    for time in range(STEPS):
        if time + rows == STEPS:
            add_panels()
        active = [x for x in reversed(range(rows)) if time + rows - x <= STEPS]

        @pl.loop(0, fields)
        def _(field):
            row_copy(time, field).wait_recv()
            for strip in strips:
                ahead = border[time, field, strip]
                for x in active:
                    later = time + rows - x
                    if x == 0:
                        value = history[later - 2, field, strip]
                    else:
                        value = state[x, field, strip]
                    ahead = advance(x, strip, value, ahead)
                    if x == 0 and later < STEPS:
                        history[later - 1, field, strip] = ahead
                    else:
                        state[x, field, strip] = ahead
            if time + rows < STEPS:
                row_copy(time + rows, field).start()
            else:
                finish(time + rows - STEPS, field)

    @pl.loop(1, n_cols)
    def _(shift):
        slot_send(shift).wait_send()

    for time in range(STEPS):

        @pl.loop(0, fields)
        def _(field):
            row_copy(time, field).wait_send()

    for x in range(rows):

        @pl.loop(0, fields)
        def _(field):
            out_copy(x, field).wait()


def per_device(
    adj_in,
    courant_x,
    courant_y,
    spread,
    corr_band,
    jacobian,
    departures,
    obs_owner,
    obs_cell,
    obs_count,
):
    rows, fields, levels, cells = adj_in.shape
    panels, field_levels, channels = jacobian.shape
    n_cols = lax.axis_size("cols")
    cap = -(-(2 * panels // n_cols) // SUB) * SUB
    slots = n_cols * cap
    width = -(-(field_levels + 1) // 128) * 128
    anywhere = pl.BlockSpec(memory_space=pl.ANY)
    f32, i32 = jnp.float32, jnp.int32
    return pl.pallas_call(
        functools.partial(window_kernel, n_cols, cap),
        out_shape=jax.ShapeDtypeStruct(adj_in.shape, f32),
        in_specs=[anywhere] * 10,
        out_specs=anywhere,
        scratch_shapes=[
            pltpu.VMEM(adj_in.shape, f32),
            pltpu.VMEM((STEPS - 1, fields, levels, cells), f32),
            pltpu.VMEM((STEPS, fields, levels, cells), f32),
            pltpu.VMEM(courant_x.shape, f32),
            pltpu.VMEM(courant_y.shape, f32),
            pltpu.VMEM(spread.shape, f32),
            pltpu.VMEM(corr_band.shape, f32),
            pltpu.VMEM(jacobian.shape, jacobian.dtype),
            pltpu.VMEM(departures.shape, departures.dtype),
            pltpu.VMEM((1, panels), i32),
            pltpu.VMEM((1, panels), i32),
            pltpu.VMEM((1, panels), i32),
            pltpu.VMEM((panels, channels), f32),
            pltpu.VMEM((panels, width), f32),
            pltpu.VMEM((slots, width), f32),
            pltpu.VMEM((slots, width), f32),
            pltpu.VMEM((rows, field_levels, cells), f32),
            pltpu.VMEM(adj_in.shape, f32),
            pltpu.SemaphoreType.DMA((rows + 9,)),
            pltpu.SemaphoreType.DMA((STEPS, fields)),
            pltpu.SemaphoreType.DMA((STEPS, fields)),
            pltpu.SemaphoreType.DMA((n_cols,)),
            pltpu.SemaphoreType.DMA((n_cols,)),
            pltpu.SemaphoreType.DMA((rows, fields)),
        ],
        compiler_params=pltpu.CompilerParams(
            collective_id=0, has_side_effects=True, vmem_limit_bytes=48 * 1024 * 1024
        ),
    )(
        adj_in,
        courant_x,
        courant_y,
        spread,
        corr_band,
        jacobian,
        departures,
        obs_owner.reshape(1, panels),
        obs_cell.reshape(1, panels),
        obs_count.reshape(1, panels),
    )


def solution(mesh):
    in_specs = (
        P(("members", "cols"), None, None, None),
        P(("members", "cols"), None, None),
        P(("members", "cols"), None, None),
        P("cols", None, None),
        P(),
        P(("members", "cols"), None, None),
        P(("members", "cols"), None),
        P(("members", "cols")),
        P(("members", "cols")),
        P(("members", "cols")),
    )
    out_specs = P(("members", "cols"), None, None, None)
    return jax.shard_map(
        per_device, mesh=mesh, in_specs=in_specs, out_specs=out_specs, check_vma=False
    )
```

time: 131 us -> 91 us (0.69)
  Pallas kernels: 0 us -> 82.3 us
  waiting for transfers between devices: 69.8 us -> 0 us
  starting transfers between devices: 17.3 us -> 0 us
  other arithmetic: 15.9 us -> 0 us
  local copies, waits for them, and re-layouts: 17.9 us -> 8.23 us
  matrix products: 8.84 us -> 0 us
    pallas_call x0 -> x1, Pallas kernels: none -> 82.3 us  [per_device(): pl.pallas_call(functools.partial(window_kernel, n_cols, cap), out_shape=j...]
    ppermute x8 -> x0, waiting for transfers between devices: 69.8 us -> none  [shifted(): return lax.ppermute(value, axis, pairs)]
    all_to_all x2 -> x0, starting transfers between devices: 15.7 us -> none  [the longest x1 7.86 us: per_device(): lax.all_to_all(send_grad.reshape(n_cols, capacity * field_levels), 'cols'...]
    add x8 -> x0, other arithmetic: 14.5 us -> none  [the longest x7 14.5 us: step_rows(): adjoint + courant_x[:, None] * (ahead - adjoint)]
    slice x31 -> x0, local copies, waits for them, and re-layouts: 9.96 us -> none  [the longest x15 5.48 us: step_rows(): ahead_y = jnp.roll(adjoint, -1, axis=3)]
    dot_general x4 -> x0, matrix products: 8.84 us -> none  [the longest x1 4.21 us: per_device(): jnp.einsum('flk,xfky->xfly', corr_band, scaled, precision=lax.Precision.H...]
    unnamed x33 -> x17, local copies, waits for them, and re-layouts: 3.63 us -> 8.23 us
    mul x3 -> x0, local copies, waits for them, and re-layouts: 2.05 us -> none  [the longest x1 1.81 us: per_device(): return spread[:, None] * mixed]
  transfers between devices with their start and end apart: 10 -> 0, of which waited for: 7 -> 0; matrix products, arithmetic and copies ran while one was open for 16% -> 0% of each run, Pallas kernels for 0% -> 0%
where the time goes in v1:
time: 91 us; the launch traced here: 90.6 us
  Pallas kernels  82.3 us (90%)
  local copies, waits for them, and re-layouts  8.23 us (9%)
    pallas_call x1, Pallas kernels, per_device(): pl.pallas_call(functools.partial(window_kernel, n_cols, cap), out_shape=j...  82.3 us
    unnamed x17, local copies, waits for them, and re-layouts  8.23 us

profile of v1, /device:TPU:29, one launch (start us, length us, event | category | flops | bytes accessed | tf_op | source)
XLA Modules:
  0.0 90.6 jit_solution(11962675424899969809)
XLA Ops:
  0.0 0.0 copy-start
  0.0 1.0 %copy-done = f32[4,32,1024]{2,1,0:T(8,128)S(1)} copy-done((f32[4,32,1024]{2,1,0:T(8,128)S(1)}, f32[4,32,1024]{2,1,0:T(8,128)}, u32[]{:S(2)}) %copy-start) | copy-done | bytes 524312
  1.0 0.0 copy-start.1
  1.0 1.0 %copy-done.1 = f32[4,32,1024]{2,1,0:T(8,128)S(1)} copy-done((f32[4,32,1024]{2,1,0:T(8,128)S(1)}, f32[4,32,1024]{2,1,0:T(8,128)}, u32[]{:S(2)}) %copy-start.1) | copy-done | bytes 524312
  2.1 0.0 copy-start.2
  2.1 1.0 %copy-done.2 = f32[4,32,1024]{2,1,0:T(8,128)S(1)} copy-done((f32[4,32,1024]{2,1,0:T(8,128)S(1)}, f32[4,32,1024]{2,1,0:T(8,128)}, u32[]{:S(2)}) %copy-start.2) | copy-done | bytes 524312
  3.1 0.0 copy-start.3
  3.1 0.9 copy-done.3
  4.0 0.0 copy-start.4
  4.0 0.8 copy-done.4
  4.8 0.0 copy-start.5
  4.8 0.7 copy-done.5
  5.4 0.0 copy-start.6
  5.4 0.7 copy-done.6
  6.1 0.0 copy-start.7
  6.1 0.7 copy-done.7
  6.7 82.3 %shard_map.100 = f32[4,5,32,1024]{3,2,1,0:T(8,128)S(1)} custom-call(f32[4,5,32,1024]{3,2,1,0:T(8,128)} %adj_hbm.1, f32[4,32,1024]{2,1,0:T(8,128)S(1)} %copy-done, f32[4,32,1024]{2,1,0:T(8,128)S(1)} %copy-done.1, f32[4,32,1024]{2,1,0:T(8,128)S(1)} %copy-done.2, f32[5,32,32]{2,1,0:T(8,128)S(1)} %copy-done.3, bf16[128,160,128]{2,1,0:T(8,128)(2,1)} %jac_hbm.1, ...), custom_call_target="tpu_custom_call" | custom-call | tf_op jit(solution)/shard_map/pallas_call | solution.py:298
  89.1 1.5 %copy.12 = f32[4,5,32,1024]{3,2,1,0:T(8,128)} copy(f32[4,5,32,1024]{3,2,1,0:T(8,128)S(1)} %shard_map.100) | data formatting | bytes 5242880
Async XLA Ops:
  0.0 1.0 %copy-start = (f32[4,32,1024]{2,1,0:T(8,128)S(1)}, f32[4,32,1024]{2,1,0:T(8,128)}, u32[]{:S(2)}) copy-start(f32[4,32,1024]{2,1,0:T(8,128)} %cx_hbm.1) | copy-start | bytes 1572868
  1.0 1.0 %copy-start.1 = (f32[4,32,1024]{2,1,0:T(8,128)S(1)}, f32[4,32,1024]{2,1,0:T(8,128)}, u32[]{:S(2)}) copy-start(f32[4,32,1024]{2,1,0:T(8,128)} %cy_hbm.1) | copy-start | bytes 1572868
  2.1 1.0 %copy-start.2 = (f32[4,32,1024]{2,1,0:T(8,128)S(1)}, f32[4,32,1024]{2,1,0:T(8,128)}, u32[]{:S(2)}) copy-start(f32[4,32,1024]{2,1,0:T(8,128)} %spread_hbm.1) | copy-start | bytes 1572868
  3.1 0.9 copy-start.3
  4.0 0.8 copy-start.4
  4.8 0.7 copy-start.5
  5.4 0.7 copy-start.6
  6.1 0.7 copy-start.7

commit v2 on v1

--- a/solution.py
+++ b/solution.py
@@ -132,7 +132,8 @@
                         history[time - 1, field, strip] = new
                     else:
                         state[x, field, strip] = new
-            row_copy(time, field).start()
+            if time < 1:
+                row_copy(time, field).start()
 
     for load in loads[rows + 2 :]:
         load.wait()
@@ -202,11 +203,24 @@
     own = pl.ds(pl.multiple_of(me * cap, SUB), cap)
     recv_slots[own, :] = send_slots[own, :]
 
+
+    @pl.loop(1, n_cols)
+    def _(shift):
+        slot_receive(shift).wait_recv()
+
+    @pl.loop(0, fields)
+    def _(field):
+        row_copy(1, field).start()
+
+    @pl.loop(0, fields)
+    def _(field):
+        row_copy(2, field).start()
+
+    @pl.loop(0, fields)
+    def _(field):
+        row_copy(3, field).start()
+
     def add_panels():
-        @pl.loop(1, n_cols)
-        def _(shift):
-            slot_receive(shift).wait_recv()
-
         received = recv_slots[...]
         target = received[:, field_levels : field_levels + 1].astype(jnp.int32) - 1
         parts = pieces(jnp.transpose(received)[0:field_levels, :])
@@ -329,7 +343,7 @@
         compiler_params=pltpu.CompilerParams(
             collective_id=0, has_side_effects=True, vmem_limit_bytes=48 * 1024 * 1024
         ),
-    )(
+    )(*[pltpu.with_memory_space_constraint(v, pltpu.HBM) for v in (
         adj_in,
         courant_x,
         courant_y,
@@ -340,6 +354,7 @@
         obs_owner.reshape(1, panels),
         obs_cell.reshape(1, panels),
         obs_count.reshape(1, panels),
+)]
     )
 
 

time: 91 us -> 75.2 us (0.83)
  the two profiles are of different devices: /device:TPU:29 before, /device:TPU:1 now
where the time goes in v2:
time: 75.2 us; the launch traced here: 75 us
  Pallas kernels  73.5 us (98%)
  local copies, waits for them, and re-layouts  1.49 us (2%)
    pallas_call x1, Pallas kernels, per_device(): pl.pallas_call(functools.partial(window_kernel, n_cols, cap), out_shape=j...  73.5 us

profile of v2, /device:TPU:1, one launch (start us, length us, event | category | flops | bytes accessed | tf_op | source)
XLA Modules:
  0.0 75.0 jit_solution(17626045583124512038)
XLA Ops:
  0.0 73.5 %shard_map.100 = f32[4,5,32,1024]{3,2,1,0:T(8,128)S(1)} custom-call(f32[4,5,32,1024]{3,2,1,0:T(8,128)} %adj_hbm.1, f32[4,32,1024]{2,1,0:T(8,128)} %cx_hbm.1, f32[4,32,1024]{2,1,0:T(8,128)} %cy_hbm.1, f32[4,32,1024]{2,1,0:T(8,128)} %spread_hbm.1, f32[5,32,32]{2,1,0:T(8,128)} %corr_hbm.1, bf16[128,160,128]{2,1,0:T(8,128)(2,1)} %jac_hbm.1, ...), custom_call_target="tpu_custom_call" | custom-call | tf_op jit(solution)/shard_map/pallas_call | solution.py:312
  73.5 1.5 %copy.12 = f32[4,5,32,1024]{3,2,1,0:T(8,128)} copy(f32[4,5,32,1024]{3,2,1,0:T(8,128)S(1)} %shard_map.100) | data formatting | bytes 5242880

commit v3 on v2

--- a/solution.py
+++ b/solution.py
@@ -204,9 +204,14 @@
     recv_slots[own, :] = send_slots[own, :]
 
 
-    @pl.loop(1, n_cols)
-    def _(shift):
-        slot_receive(shift).wait_recv()
+    patient = me == 0
+
+    def wait_for_slots():
+        @pl.loop(1, n_cols)
+        def _(shift):
+            slot_receive(shift).wait_recv()
+
+    pl.when(patient)(wait_for_slots)
 
     @pl.loop(0, fields)
     def _(field):
@@ -221,6 +226,7 @@
         row_copy(3, field).start()
 
     def add_panels():
+        pl.when(jnp.logical_not(patient))(wait_for_slots)
         received = recv_slots[...]
         target = received[:, field_levels : field_levels + 1].astype(jnp.int32) - 1
         parts = pieces(jnp.transpose(received)[0:field_levels, :])

time: 75.2 us -> 72.4 us (0.963)
  the two profiles are of different devices: /device:TPU:1 before, /device:TPU:29 now
where the time goes in v3:
time: 72.4 us; the launch traced here: 72.3 us
  Pallas kernels  70.8 us (98%)
  local copies, waits for them, and re-layouts  1.49 us (2%)
    pallas_call x1, Pallas kernels, per_device(): pl.pallas_call(functools.partial(window_kernel, n_cols, cap), out_shape=j...  70.8 us
    unnamed x1, local copies, waits for them, and re-layouts  1.49 us

profile of v3, /device:TPU:29, one launch (start us, length us, event | category | flops | bytes accessed | tf_op | source)
XLA Modules:
  0.0 72.3 jit_solution(6583057581842751292)
XLA Ops:
  0.0 70.8 %shard_map.100 = f32[4,5,32,1024]{3,2,1,0:T(8,128)S(1)} custom-call(f32[4,5,32,1024]{3,2,1,0:T(8,128)} %adj_hbm.1, f32[4,32,1024]{2,1,0:T(8,128)} %cx_hbm.1, f32[4,32,1024]{2,1,0:T(8,128)} %cy_hbm.1, f32[4,32,1024]{2,1,0:T(8,128)} %spread_hbm.1, f32[5,32,32]{2,1,0:T(8,128)} %corr_hbm.1, bf16[128,160,128]{2,1,0:T(8,128)(2,1)} %jac_hbm.1, ...), custom_call_target="tpu_custom_call" | custom-call | tf_op jit(solution)/shard_map/pallas_call | solution.py:318
  70.8 1.5 %copy.12 = f32[4,5,32,1024]{3,2,1,0:T(8,128)} copy(f32[4,5,32,1024]{3,2,1,0:T(8,128)S(1)} %shard_map.100) | data formatting | bytes 5242880

commit v4 on v3

--- a/solution.py
+++ b/solution.py
@@ -59,7 +59,9 @@
 ):
     rows, fields, levels, cells = state.shape
     panels, field_levels, channels = jac.shape
-    slots, width = send_slots.shape
+    slots, width = n_cols * cap, grad.shape[1]
+    fold = 2 if cap % (2 * SUB) == 0 else 1
+    short = cap // fold
     me = lax.axis_index("cols")
     left = lax.rem(me + n_cols - 1, n_cols)
 
@@ -172,10 +174,18 @@
         jnp.dot(chosen, piece, preferred_element_type=jnp.float32) for piece in pieces(grad[...])
     )
     column = lax.broadcasted_iota(jnp.int32, (slots, width), 1)
-    send_slots[...] = jnp.where(column == field_levels, placing_cell, placed)
+    placed = jnp.where(column == field_levels, placing_cell, placed)
+    wide = placed[:, 0:128].reshape(n_cols, cap, 128)
+    rest = placed[:, 128:256]
+    if fold == 2:
+        pairs = rest.reshape(n_cols, 2, short, 128)
+        upper = pltpu.roll(pairs[:, 1].reshape(n_cols * short, 128), 64, 1)
+        rest = pairs[:, 0].reshape(n_cols * short, 128) + upper
+    send_slots[:, 0:cap, :] = wide
+    send_slots[:, cap : cap + short, :] = rest.reshape(n_cols, short, 128)
 
     def slot_block(ref, device):
-        return ref.at[pl.ds(pl.multiple_of(device * cap, SUB), cap), :]
+        return ref.at[device]
 
     def slot_send(shift):
         target = lax.rem(me + shift, n_cols)
@@ -200,8 +210,7 @@
     def _(shift):
         slot_send(shift).start()
 
-    own = pl.ds(pl.multiple_of(me * cap, SUB), cap)
-    recv_slots[own, :] = send_slots[own, :]
+    recv_slots[me] = send_slots[me]
 
 
     patient = me == 0
@@ -227,7 +236,13 @@
 
     def add_panels():
         pl.when(jnp.logical_not(patient))(wait_for_slots)
-        received = recv_slots[...]
+        rest = recv_slots[:, cap : cap + short, :]
+        if fold == 2:
+            upper = pltpu.roll(rest.reshape(n_cols * short, 128), 64, 1)
+            rest = jnp.concatenate([rest, upper.reshape(n_cols, short, 128)], axis=1)
+        received = jnp.concatenate(
+            [recv_slots[:, 0:cap, :].reshape(slots, 128), rest.reshape(slots, 128)], axis=1
+        )
         target = received[:, field_levels : field_levels + 1].astype(jnp.int32) - 1
         parts = pieces(jnp.transpose(received)[0:field_levels, :])
         for x in range(rows):
@@ -311,7 +326,7 @@
     panels, field_levels, channels = jacobian.shape
     n_cols = lax.axis_size("cols")
     cap = -(-(2 * panels // n_cols) // SUB) * SUB
-    slots = n_cols * cap
+    short = cap // 2 if cap % (2 * SUB) == 0 else cap
     width = -(-(field_levels + 1) // 128) * 128
     anywhere = pl.BlockSpec(memory_space=pl.ANY)
     f32, i32 = jnp.float32, jnp.int32
@@ -335,8 +350,8 @@
             pltpu.VMEM((1, panels), i32),
             pltpu.VMEM((panels, channels), f32),
             pltpu.VMEM((panels, width), f32),
-            pltpu.VMEM((slots, width), f32),
-            pltpu.VMEM((slots, width), f32),
+            pltpu.VMEM((n_cols, cap + short, 128), f32),
+            pltpu.VMEM((n_cols, cap + short, 128), f32),
             pltpu.VMEM((rows, field_levels, cells), f32),
             pltpu.VMEM(adj_in.shape, f32),
             pltpu.SemaphoreType.DMA((rows + 9,)),

time: 72.4 us -> 71.5 us (0.988)
  Pallas kernels: 70.8 us -> 69.9 us
    pallas_call x1, Pallas kernels: 70.8 us -> 69.9 us  [per_device(): pl.pallas_call(functools.partial(window_kernel, n_cols, cap), out_shape=j...]
where the time goes in v4:
time: 71.5 us; the launch traced here: 71.4 us
  Pallas kernels  69.9 us (98%)
  local copies, waits for them, and re-layouts  1.49 us (2%)
    pallas_call x1, Pallas kernels, per_device(): pl.pallas_call(functools.partial(window_kernel, n_cols, cap), out_shape=j...  69.9 us
    unnamed x1, local copies, waits for them, and re-layouts  1.49 us

profile of v4, /device:TPU:29, one launch (start us, length us, event | category | flops | bytes accessed | tf_op | source)
XLA Modules:
  0.0 71.4 jit_solution(8389848462761591268)
XLA Ops:
  0.0 69.9 %shard_map.100 = f32[4,5,32,1024]{3,2,1,0:T(8,128)S(1)} custom-call(f32[4,5,32,1024]{3,2,1,0:T(8,128)} %adj_hbm.1, f32[4,32,1024]{2,1,0:T(8,128)} %cx_hbm.1, f32[4,32,1024]{2,1,0:T(8,128)} %cy_hbm.1, f32[4,32,1024]{2,1,0:T(8,128)} %spread_hbm.1, f32[5,32,32]{2,1,0:T(8,128)} %corr_hbm.1, bf16[128,160,128]{2,1,0:T(8,128)(2,1)} %jac_hbm.1, ...), custom_call_target="tpu_custom_call" | custom-call | tf_op jit(solution)/shard_map/pallas_call | solution.py:333
  69.9 1.5 %copy.12 = f32[4,5,32,1024]{3,2,1,0:T(8,128)} copy(f32[4,5,32,1024]{3,2,1,0:T(8,128)S(1)} %shard_map.100) | data formatting | bytes 5242880
